TPU v7x, 32 devices: a whole 2x2x4 slice. The times are simulated.
32 devices in a mesh: outer: 2 (over x), sec: 8 (over z, core), tp: 2 (over y).
Axes of the slice: x: 2, y: 2, z: 4, core: 2. Of those that a mesh axis runs over, the one named last changes fastest.
Arguments:
- tile_maps: bfloat16 [32, 12, 12, 3072], P(('outer', 'sec'), None, None, 'tp'), may hold values from -6 to 6
- tile_shape: int32 [32, 2], P(('outer', 'sec')), may hold values from 4 to 12
- conv_kernel: float32 [7, 7, 3072], P(None, None, 'tp'), may hold values from -0.875 to 0.875
- norm_gain: float32 [3072], P('tp'), may hold values from 0.25 to 1.75
- norm_bias: float32 [3072], P('tp'), may hold values from -3 to 3
- projector: bfloat16 [3072, 7168], P('tp', 'sec'), may hold values from -0.109375 to 0.109375
- text_rows: bfloat16 [9216, 7168], P(('outer', 'sec'), 'tp'), may hold values from -6 to 6
- row_order: int32 [16, 576], P(('outer', 'sec')), may hold values from 0 to 575, each once within a row
- seq_gain: float32 [7168], P('tp'), may hold values from 0.25 to 1.75
- cotangent: bfloat16 [9216, 7168], P(('outer', 'sec'), 'tp'), may hold values from -0.2772166 to 0.2772166, as said below
Outputs:
- normed: bfloat16 [9216, 7168], P(('outer', 'sec'), 'tp')
- kernel_delta: float32 [7, 7, 3072], P(None, None, 'tp')
- gain_delta: float32 [3072], P('tp')
- bias_delta: float32 [3072], P('tp')
Inputs may be any that keep to these rules, and one draw needn't show every extreme that they name: `row_order`: each row lists where the visual tokens arriving at that device stand, in arrival order, then the text rows. `tile_shape`: valid rows and columns of each tile, the rest of the map is padding. `cotangent`: gradient of the training loss.
All inputs are finite; a program needn't handle non-finite values.
Results may differ from a plain program's by a relative error of at most 0.0043.
Values may be sent and summed in bfloat16 or wider, within the bound.
A program may use at most 128 MiB of HBM per device.

v0:
```python
import jax
import jax.numpy as jnp
from jax import lax
from jax.sharding import PartitionSpec as P


def shape_mask(tile_shape, grid):
    places = lax.broadcasted_iota(jnp.int32, (1, grid), 1)
    rows_ok = places < tile_shape[:, 0:1]
    cols_ok = places < tile_shape[:, 1:2]
    return (rows_ok[:, :, None] & cols_ok[:, None, :]).astype(jnp.float32)


def on_device(
    tile_maps,
    tile_shape,
    conv_kernel,
    norm_gain,
    norm_bias,
    projector,
    text_rows,
    row_order,
    seq_gain,
    cotangent,
):
    grid = tile_maps.shape[1]
    half_ch = tile_maps.shape[3]
    channels = half_ch * lax.axis_size("tp")
    rows_dev = tile_maps.shape[0] * grid * grid
    width = text_rows.shape[1] * lax.axis_size("tp")
    validity = shape_mask(tile_shape, grid)[..., None]
    masked = tile_maps.astype(jnp.float32) * validity
    padded = jnp.pad(masked, ((0, 0), (3, 3), (3, 3), (0, 0)))
    conv_out = jnp.zeros(masked.shape, jnp.float32)
    for row_off in range(7):
        for col_off in range(7):
            conv_out = (
                conv_out
                + padded[:, row_off : row_off + grid, col_off : col_off + grid, :]
                * conv_kernel[row_off, col_off]
            )
    total_one, total_two = lax.psum(
        (jnp.sum(conv_out, axis=-1), jnp.sum(conv_out * conv_out, axis=-1)), "tp"
    )
    center = (total_one / channels)[..., None]
    inverse = lax.rsqrt((total_two / channels)[..., None] - center * center + 1e-06)
    normal = (conv_out - center) * inverse
    features = (
        (validity * (normal * norm_gain + norm_bias))
        .astype(jnp.bfloat16)
        .reshape(rows_dev, half_ch)
    )
    whole_weight = lax.all_gather(projector, "sec", axis=1, tiled=True)
    partial_value = jnp.dot(features, whole_weight, preferred_element_type=jnp.float32)
    visual = lax.psum_scatter(partial_value, "tp", scatter_dimension=1, tiled=True).astype(
        jnp.bfloat16
    )
    arrived = lax.all_to_all(visual, "sec", split_axis=0, concat_axis=0, tiled=True)
    positions = row_order[0, :rows_dev]
    merged = text_rows.at[positions].set(arrived)
    wide = merged.astype(jnp.float32)
    upstream = cotangent.astype(jnp.float32) * seq_gain
    square_sum, along = lax.psum(
        (jnp.sum(wide * wide, axis=-1), jnp.sum(upstream * wide, axis=-1)), "tp"
    )
    inv_rms = lax.rsqrt(square_sum / width + 1e-05)[:, None]
    normed = (wide * inv_rms * seq_gain).astype(jnp.bfloat16)
    grad_seq = inv_rms * upstream - wide * (inv_rms * inv_rms * inv_rms) * along[:, None] / width
    picked = grad_seq[positions].astype(jnp.bfloat16)
    returned = lax.all_to_all(picked, "sec", split_axis=0, concat_axis=0, tiled=True)
    full_grad = lax.all_gather(returned, "tp", axis=1, tiled=True)
    grad_rows = jnp.dot(full_grad, whole_weight.T, preferred_element_type=jnp.float32)
    masked_grad = grad_rows.reshape(masked.shape) * validity
    scaled = masked_grad * norm_gain
    first_sum, second_sum = lax.psum(
        (jnp.sum(scaled, axis=-1), jnp.sum(scaled * normal, axis=-1)), "tp"
    )
    grad_conv = inverse * (
        scaled - (first_sum / channels)[..., None] - normal * (second_sum / channels)[..., None]
    )
    kernel_rows = []
    for row_off in range(7):
        for col_off in range(7):
            window = padded[:, row_off : row_off + grid, col_off : col_off + grid, :]
            kernel_rows.append(jnp.sum(window * grad_conv, axis=(0, 1, 2)))
    gain_grad = jnp.sum(masked_grad * normal, axis=(0, 1, 2))
    bias_grad = jnp.sum(masked_grad, axis=(0, 1, 2))
    local_delta = jnp.stack(kernel_rows + [gain_grad, bias_grad], axis=0)
    pods = lax.axis_size("outer")
    entries = 51 * channels
    pod_sum = lax.psum(local_delta, "sec")
    norm_sq = lax.psum(jnp.sum(pod_sum * pod_sum), "tp")
    factor = jnp.minimum(1.0, 1.0 / jnp.sqrt(norm_sq / entries + 1e-06))
    average = lax.psum(pod_sum * factor, "outer") / pods
    return (normed, average[:49].reshape(7, 7, half_ch), average[49], average[50])


def solution(mesh):
    in_specs = (
        P(("outer", "sec"), None, None, "tp"),
        P(("outer", "sec"), None),
        P(None, None, "tp"),
        P("tp"),
        P("tp"),
        P("tp", "sec"),
        P(("outer", "sec"), "tp"),
        P(("outer", "sec"), None),
        P("tp"),
        P(("outer", "sec"), "tp"),
    )
    out_specs = (P(("outer", "sec"), "tp"), P(None, None, "tp"), P("tp"), P("tp"))
    return jax.shard_map(
        on_device, mesh=mesh, in_specs=in_specs, out_specs=out_specs, check_vma=False
    )
```

profile of v0, /device:TPU:0, one launch (start us, length us, event | category | flops | bytes accessed | tf_op | source)
XLA Modules:
  0.0 696.8 jit_solution(15552070662868830435)
XLA Ops:
  14.4 23.6 %fusion.8 = (f32[2,12,12]{2,1,0:T(8,128)S(1)}, f32[2,12,12]{2,1,0:T(8,128)S(1)}, f32[2,12,12,1536]{3,2,1,0:T(8,128)}) fusion(f32[1536]{0:T(1024)S(1)} %get-tuple-element.110, f32[1536]{0:T(1024)S(1)} %get-tuple-element.111, f32[1536]{0:T(1024)S(1)} %get-tuple-element.64, f32[1536]{0:T(1024)S(1)} %get-tuple-element.65, f32[1536]{0:T(1024)S(1)} %get-tuple-element.66, ...), kind=kLoop, calls=%fused_computation.189 | loop fusion | flops 44236224 | bytes 3842304 | tf_op jit(solution)/shard_map/reduce_sum | solution.py:43
  38.1 9.8 %all-reduce.3 = (f32[2,12,12]{2,1,0:T(8,128)S(1)}, f32[2,12,12]{2,1,0:T(8,128)S(1)}) all-reduce(f32[2,12,12]{2,1,0:T(8,128)S(1)} %get-tuple-element.58, f32[2,12,12]{2,1,0:T(8,128)S(1)} %get-tuple-element.57), channel_id=1, replica_groups=mesh['outer'=2,'sec'=8,'tp'=2] {'tp'}, use_global_device_ids=true, to_apply=%region_3.4 | all-reduce | flops 576 | bytes 4608 | tf_op jit(solution)/shard_map/psum | solution.py:42
  53.1 155.4 %all-gather.3.cloned.1.call-done = bf16[1536,7168]{1,0:T(8,128)(2,1)} async-done(((bf16[1536,896]{1,0:T(8,128)(2,1)}), bf16[1536,7168]{1,0:T(8,128)(2,1)}) %all-gather.3.cloned.1.call-update) | async-done | bytes 22020112 | tf_op jit(solution)/shard_map/all_gather | solution.py:53
  208.5 13.1 %fusion.9 = f32[288,7168]{1,0:T(8,128)} fusion(bf16[288,1536]{1,0:T(8,128)(2,1)} %reshape.168, bf16[1536,7168]{1,0:T(8,128)(2,1)} %all-gather.3.cloned.1.call-done), kind=kOutput, calls=%fused_computation.190 | convolution fusion | flops 6341787648 | bytes 31162368 | tf_op jit(solution)/shard_map/dot_general | solution.py:54
  221.7 96.2 %reduce-scatter.2.cloned.1.call-done = f32[288,3584]{1,0:T(8,128)} async-done(((f32[288,7168]{1,0:T(8,128)}), f32[288,3584]{1,0:T(8,128)}) %reduce-scatter.2.cloned.1.call-update) | async-done | bytes 4128784 | tf_op jit(solution)/shard_map/reduce_scatter | solution.py:55
  325.5 4.7 all-to-all-start
  330.5 53.1 %all-to-all-done = bf16[8,36,3584]{2,1,0:T(8,128)(2,1)} async-done(((bf16[8,36,3584]{2,1,0:T(8,128)(2,1)}), bf16[8,36,3584]{2,1,0:T(8,128)(2,1)}, u32[]{:S(2)}, u32[]{:S(2)}) %all-to-all-start) | async-done | bytes 2064416 | tf_op jit(solution)/shard_map/all_to_all | solution.py:58
  387.7 9.2 %scatter_fusion = bf16[576,3584]{1,0:T(8,128)(2,1)} fusion(bf16[576,3584]{1,0:T(8,128)(2,1)} %copy.23, s32[288]{0:T(512)S(1)} %fusion.7, bf16[288,3584]{1,0:T(8,128)(2,1)} %reshape.184), kind=kCustom, calls=%fused_computation.1 | custom fusion | bytes 6194304 | tf_op jit(solution)/shard_map/scatter | solution.py:60
  396.9 5.4 fusion.6
  402.3 5.0 all-reduce.2
  407.3 6.7 fusion.5
  414.0 10.0 %gather_fusion = bf16[288,3584]{1,0:T(8,128)(2,1)} fusion(bf16[576,3584]{1,0:T(8,128)(2,1)} %fusion.5, s32[1024]{0:T(1024)S(1)} %pad_clamp_fusion), kind=kCustom, calls=%fused_computation | custom fusion | bytes 4129920 | tf_op jit(solution)/shard_map/gather | solution.py:69
  428.0 57.6 %all_to_all.21 = bf16[8,36,3584]{2,1,0:T(8,128)(2,1)} all-to-all(bf16[8,36,3584]{2,1,0:T(8,128)(2,1)} %convert_element_type.48), channel_id=1, replica_groups=mesh['outer'=2,'sec'=8,'tp'=2] {'sec'}, dimensions={0} | all-to-all | bytes 4128768 | tf_op jit(solution)/shard_map/all_to_all | solution.py:70
  489.8 54.0 %all-gather.5.cloned.1.call-done = bf16[288,7168]{1,0:T(8,128)(2,1)} async-done(((bf16[288,3584]{1,0:T(8,128)(2,1)}), bf16[288,7168]{1,0:T(8,128)(2,1)}) %all-gather.5.cloned.1.call-update) | async-done | bytes 4128784 | tf_op jit(solution)/shard_map/all_gather | solution.py:71
  543.7 13.2 %multiply_reduce_fusion.53 = (f32[1536]{0:T(1024)S(1)}, f32[288]{0:T(512)S(1)}, f32[288,1536]{1,0:T(8,128)}) fusion(f32[288]{0:T(512)S(1)} %reshape.171, f32[1536]{0:T(1024)S(1)} %copy-done.8, bf16[288,7168]{1,0:T(8,128)(2,1)} %all-gather.5.cloned.1.call-done, bf16[1536,7168]{1,0:T(8,128)(2,1)} %all-gather.3.cloned.1.call-done), kind=kOutput, calls=%fused_computation.120 | convolution fusion | flops 6343555072 | bytes 27932928 | tf_op jit(solution)/shard_map/dot_general | solution.py:72
  563.2 7.4 %all-reduce.1 = (f32[2,12,12]{2,1,0:T(8,128)S(1)}, f32[2,12,12]{2,1,0:T(8,128)S(1)}) all-reduce(f32[2,12,12]{2,1,0:T(8,128)S(1)} %get-tuple-element.5, f32[2,12,12]{2,1,0:T(8,128)S(1)} %reduce_sum.529), channel_id=1, replica_groups=mesh['outer'=2,'sec'=8,'tp'=2] {'tp'}, use_global_device_ids=true, to_apply=%region_13.14 | all-reduce | flops 576 | bytes 4608 | tf_op jit(solution)/shard_map/psum | solution.py:75
  570.7 9.6 %multiply_reduce_fusion.1 = (f32[1536]{0:T(1024)S(1)}, f32[1536]{0:T(1024)S(1)}, f32[1536]{0:T(1024)S(1)}, f32[1536]{0:T(1024)S(1)}, f32[1536]{0:T(1024)S(1)}, /...) fusion(f32[2,12,12,1536]{3,2,1,0:T(8,128)S(1)} %convert_multipl, ...), kind=kLoop, calls=%fused_computation.63 | loop fusion | flops 19436544 | bytes 7200384 | tf_op jit(solution)/shard_map/reduce_sum | solution.py:85
  580.3 6.3 multiply_reduce_fusion.19
  586.6 5.4 multiply_reduce_fusion.38
  592.8 4.8 stack.207
  597.7 54.4 %all-reduce.7.cloned.1.call-done = f32[51,1536]{1,0:T(8,128)} async-done(((f32[51,1536]{1,0:T(8,128)}), f32[51,1536]{1,0:T(8,128)}) %all-reduce.7.cloned.1.call-update) | async-done | bytes 313360 | tf_op jit(solution)/shard_map/psum | solution.py:91
  653.7 5.5 psum.70
  661.7 5.5 fusion.2
  667.2 20.6 %all-reduce.9.cloned.1.call-done = f32[51,1536]{1,0:T(8,128)} async-done(((f32[51,1536]{1,0:T(8,128)}), f32[51,1536]{1,0:T(8,128)}) %all-reduce.9.cloned.1.call-update) | async-done | bytes 313360 | tf_op jit(solution)/shard_map/psum | solution.py:94
  (113 shorter events, 44.9 us)
Async XLA Ops:
  7.2 201.4 %all-gather.3.cloned.1.call-start = ((), (), s32[]{:S(2)}) async-start(), calls=%async_computation.3 | async-start | bytes 24772608 | tf_op jit(solution)/shard_map/all_gather | solution.py:53
  11.6 0.7 copy-start.9
  11.6 1.0 copy-start.2
  11.6 2.6 copy-start
  11.7 306.2 %reduce-scatter.2.cloned.1.call-start = ((), (), s32[]{:S(2)}) async-start(), calls=%async_computation.4 | async-start | bytes 12386304 | tf_op jit(solution)/shard_map/reduce_scatter | solution.py:55
  47.9 0.6 copy-start.3
  47.9 0.6 copy-start.5
  325.5 5.0 copy-start.10
  325.5 58.1 %all-to-all-start = ((bf16[8,36,3584]{2,1,0:T(8,128)(2,1)}), bf16[8,36,3584]{2,1,0:T(8,128)(2,1)}, u32[]{:S(2)}, u32[]{:S(2)}) async-start(bf16[8,36,3584]{2,1,0:T(8,128)(2,1)} %all_to_all.14), calls=%async_computation.1 | async-start | bytes 4587520 | tf_op jit(solution)/shard_map/all_to_all | solution.py:58
  330.3 213.5 %all-gather.5.cloned.1.call-start = ((), (), s32[]{:S(2)}) async-start(), calls=%async_computation.5 | async-start | bytes 6193152 | tf_op jit(solution)/shard_map/all_gather | solution.py:71
  387.7 9.2 %copy-start.7 = (f32[3584]{0:T(1024)S(1)}, f32[3584]{0:T(1024)}, u32[]{:S(2)}) copy-start(f32[3584]{0:T(1024)} %param.18) | copy-start | bytes 43012
  485.6 58.1 %copy-start.8 = (f32[1536]{0:T(1024)S(1)}, f32[1536]{0:T(1024)}, u32[]{:S(2)}) copy-start(f32[1536]{0:T(1024)} %param.13) | copy-start | bytes 18436
  489.6 162.4 %all-reduce.7.cloned.1.call-start = ((), (), s32[]{:S(2)}) async-start(), calls=%async_computation.6 | async-start | bytes 688128 | tf_op jit(solution)/shard_map/psum | solution.py:91
  557.0 2.8 copy-start.4
  557.0 2.8 copy-start.6
  580.3 6.4 copy-start.1
  597.6 90.2 %all-reduce.9.cloned.1.call-start = ((), (), s32[]{:S(2)}) async-start(), calls=%async_computation.7 | async-start | bytes 688128 | tf_op jit(solution)/shard_map/psum | solution.py:94
Sparse Core Ops, SparseCore 0:
  11.8 196.7 all-gather.2
  221.8 96.0 reduce-scatter.1
  489.8 53.9 all-gather.4
  597.7 54.2 all-reduce.6
  661.8 25.9 all-reduce.8
where the time goes:
time: 698 us; the launch traced here: 697 us
  waiting for transfers between devices  434 us (62%)
  blocking collectives  85.4 us (12%)
  other arithmetic  78 us (11%)
  local copies, waits for them, and re-layouts  53.2 us (8%)
  matrix products  26.4 us (4%)
  between operations  15 us (2%)
    all_gather x1, waiting for transfers between devices, on_device(): whole_weight = lax.all_gather(projector, 'sec', axis=1, tiled=True)  155 us
    reduce_scatter x1, waiting for transfers between devices, on_device(): lax.psum_scatter(partial_value, 'tp', scatter_dimension=1, tiled=True)  96.2 us
    all_to_all x1, blocking collectives, on_device(): lax.all_to_all(picked, 'sec', split_axis=0, concat_axis=0, tiled=True)  57.6 us
    psum x1, waiting for transfers between devices, on_device(): pod_sum = lax.psum(local_delta, 'sec')  54.4 us
    all_gather x1, waiting for transfers between devices, on_device(): full_grad = lax.all_gather(returned, 'tp', axis=1, tiled=True)  54 us
    all_to_all x1, waiting for transfers between devices, on_device(): lax.all_to_all(visual, 'sec', split_axis=0, concat_axis=0, tiled=True)  53.1 us
    reduce_sum x1, other arithmetic, on_device(): jnp.sum(conv_out, axis=-1)  23.6 us
    reduce_sum x3, other arithmetic, on_device(): kernel_rows.append(jnp.sum(window * grad_conv, axis=(0, 1, 2)))  21.3 us
  transfers between devices with their start and end apart: 6, of which 6 were waited for; matrix products, arithmetic and copies ran while one was open for 5% of the time, Pallas kernels for 0%

commit v1 on v0

--- a/solution.py
+++ b/solution.py
@@ -50,7 +50,16 @@
         .astype(jnp.bfloat16)
         .reshape(rows_dev, half_ch)
     )
-    whole_weight = lax.all_gather(projector, "sec", axis=1, tiled=True)
+    ways = lax.axis_size("sec")
+    up = [(d, (d + 1) % ways) for d in range(ways)]
+    down = [(d, (d - 1) % ways) for d in range(ways)]
+    earlier, later = ([projector], [projector])
+    for _ in range(ways // 2):
+        earlier.append(lax.ppermute(earlier[-1], "sec", up))
+    for _ in range((ways - 1) // 2):
+        later.append(lax.ppermute(later[-1], "sec", down))
+    line = jnp.concatenate([*earlier[::-1], *later[1:]], axis=1)
+    whole_weight = jnp.roll(line, (lax.axis_index("sec") - ways // 2) * projector.shape[1], axis=1)
     partial_value = jnp.dot(features, whole_weight, preferred_element_type=jnp.float32)
     visual = lax.psum_scatter(partial_value, "tp", scatter_dimension=1, tiled=True).astype(
         jnp.bfloat16

time: 698 us -> 771 us (1.10)
  local copies, waits for them, and re-layouts: 53.2 us -> 111 us
  starting transfers between devices: 5.12 us -> 14.9 us
    all_gather x1 -> x0, waiting for transfers between devices: 155 us -> none  [on_device(): whole_weight = lax.all_gather(projector, 'sec', axis=1, tiled=True)]
    ppermute x0 -> x7, waiting for transfers between devices: none -> 150 us  [the longest x4 148 us: on_device(): earlier.append(lax.ppermute(earlier[-1], 'sec', up))]
    unnamed x23 -> x42, local copies, waits for them, and re-layouts: 5.79 us -> 57 us
    ppermute x0 -> x7, starting transfers between devices: none -> 9.46 us  [the longest x3 9 us: on_device(): later.append(lax.ppermute(later[-1], 'sec', down))]
  transfers between devices with their start and end apart: 6 -> 12, of which waited for: 6 -> 9; matrix products, arithmetic and copies ran while one was open for 5% -> 8% of each run, Pallas kernels for 0% -> 0%
where the time goes in v1:
time: 771 us; the launch traced here: 765 us
  waiting for transfers between devices  431 us (56%)
  local copies, waits for them, and re-layouts  111 us (14%)
  blocking collectives  86.6 us (11%)
  other arithmetic  76.3 us (10%)
  matrix products  29.5 us (4%)
  between operations  15.3 us (2%)
  starting transfers between devices  14.9 us (2%)
    ppermute x4, waiting for transfers between devices, on_device(): earlier.append(lax.ppermute(earlier[-1], 'sec', up))  148 us
    reduce_scatter x1, waiting for transfers between devices, on_device(): lax.psum_scatter(partial_value, 'tp', scatter_dimension=1, tiled=True)  98.7 us
    all_to_all x1, blocking collectives, on_device(): lax.all_to_all(picked, 'sec', split_axis=0, concat_axis=0, tiled=True)  57.6 us
    unnamed x42, local copies, waits for them, and re-layouts  57 us
    psum x1, waiting for transfers between devices, on_device(): pod_sum = lax.psum(local_delta, 'sec')  54.4 us
    all_gather x1, waiting for transfers between devices, on_device(): full_grad = lax.all_gather(returned, 'tp', axis=1, tiled=True)  54 us
    all_to_all x1, waiting for transfers between devices, on_device(): lax.all_to_all(visual, 'sec', split_axis=0, concat_axis=0, tiled=True)  52.8 us
    reduce_sum x1, other arithmetic, on_device(): jnp.sum(conv_out, axis=-1)  22 us
  transfers between devices with their start and end apart: 12, of which 9 were waited for; matrix products, arithmetic and copies ran while one was open for 8% of the time, Pallas kernels for 0%

profile of v1, /device:TPU:0, one launch (start us, length us, event | category | flops | bytes accessed | tf_op | source)
XLA Modules:
  0.0 764.8 jit_solution(1421490677734513257)
XLA Ops:
  12.2 35.0 %collective-permute-done = bf16[1536,896]{1,0:T(8,128)(2,1)S(1)} collective-permute-done((bf16[1536,896]{1,0:T(8,128)(2,1)}, bf16[1536,896]{1,0:T(8,128)(2,1)S(1)}, u32[]{:S(2)}, u32[]{:S(2)}) %collective-permute-start) | collective-permute-done | bytes 2752544 | tf_op jit(solution)/shard_map/ppermute | solution.py:58
  52.2 59.4 %collective-permute-done.1 = bf16[1536,896]{1,0:T(8,128)(2,1)} collective-permute-done((bf16[1536,896]{1,0:T(8,128)(2,1)S(1)}, bf16[1536,896]{1,0:T(8,128)(2,1)}, u32[]{:S(2)}, u32[]{:S(2)}) %collective-permute-start.1) | collective-permute-done | bytes 2752544 | tf_op jit(solution)/shard_map/ppermute | solution.py:58
  120.7 53.2 %collective-permute-done.2 = bf16[1536,896]{1,0:T(8,128)(2,1)} collective-permute-done((bf16[1536,896]{1,0:T(8,128)(2,1)}, bf16[1536,896]{1,0:T(8,128)(2,1)}, u32[]{:S(2)}, u32[]{:S(2)}) %collective-permute-start.2) | collective-permute-done | bytes 2752544 | tf_op jit(solution)/shard_map/ppermute | solution.py:58
  173.9 22.0 %fusion.14 = (f32[2,12,12]{2,1,0:T(8,128)S(1)}, f32[2,12,12]{2,1,0:T(8,128)S(1)}, f32[2,12,12,1536]{3,2,1,0:T(8,128)}) fusion(f32[1536]{0:T(1024)S(1)} %get-tuple-element.110, f32[1536]{0:T(1024)S(1)} %get-tuple-element.111, f32[1536]{0:T(1024)S(1)} %get-tuple-element.64, f32[1536]{0:T(1024)S(1)} %get-tuple-element.65, f32[1536]{0:T(1024)S(1)} %get-tuple-element.66, ...), kind=kLoop, calls=%fused_computation.211 | loop fusion | flops 44236224 | bytes 3842304 | tf_op jit(solution)/shard_map/reduce_sum | solution.py:43
  195.9 10.9 %all-reduce.3 = (f32[2,12,12]{2,1,0:T(8,128)S(1)}, f32[2,12,12]{2,1,0:T(8,128)S(1)}) all-reduce(f32[2,12,12]{2,1,0:T(8,128)S(1)} %get-tuple-element.58, f32[2,12,12]{2,1,0:T(8,128)S(1)} %get-tuple-element.57), channel_id=1, replica_groups=mesh['outer'=2,'sec'=8,'tp'=2] {'tp'}, use_global_device_ids=true, to_apply=%region_3.4 | all-reduce | flops 576 | bytes 4608 | tf_op jit(solution)/shard_map/psum | solution.py:42
  270.5 14.1 %fusion.2 = f32[288,7168]{1,0:T(8,128)} fusion(bf16[288,1536]{1,0:T(8,128)(2,1)S(1)} %copy-done.4, bf16[1536,14336]{1,0:T(8,128)(2,1)} %constant_dynamic-update-slice_fusion, s32[]{:T(128)S(6)} %select_n.26), kind=kOutput, calls=%fused_computation.52 | convolution fusion | flops 6341787648 | bytes 31162372 | tf_op jit(solution)/shard_map/dot_general | solution.py:63
  284.6 98.7 %reduce-scatter.2.cloned.1.call-done = f32[288,3584]{1,0:T(8,128)} async-done(((f32[288,7168]{1,0:T(8,128)}), f32[288,3584]{1,0:T(8,128)}) %reduce-scatter.2.cloned.1.call-update) | async-done | bytes 4128784 | tf_op jit(solution)/shard_map/reduce_scatter | solution.py:64
  396.3 52.8 %all-to-all-done = bf16[8,36,3584]{2,1,0:T(8,128)(2,1)} async-done(((bf16[8,36,3584]{2,1,0:T(8,128)(2,1)}), bf16[8,36,3584]{2,1,0:T(8,128)(2,1)}, u32[]{:S(2)}, u32[]{:S(2)}) %all-to-all-start) | async-done | bytes 2064416 | tf_op jit(solution)/shard_map/all_to_all | solution.py:67
  453.1 9.2 %scatter_fusion = bf16[576,3584]{1,0:T(8,128)(2,1)} fusion(bf16[576,3584]{1,0:T(8,128)(2,1)} %copy.38, s32[288]{0:T(512)S(1)} %fusion.11, bf16[288,3584]{1,0:T(8,128)(2,1)} %reshape.184), kind=kCustom, calls=%fused_computation.1 | custom fusion | bytes 6194304 | tf_op jit(solution)/shard_map/scatter | solution.py:69
  462.3 5.4 fusion.10
  467.7 5.2 all-reduce.2
  472.8 6.7 fusion.9
  479.5 10.0 %gather_fusion = bf16[288,3584]{1,0:T(8,128)(2,1)} fusion(bf16[576,3584]{1,0:T(8,128)(2,1)} %fusion.9, s32[1024]{0:T(1024)S(1)} %pad_clamp_fusion), kind=kCustom, calls=%fused_computation | custom fusion | bytes 4129920 | tf_op jit(solution)/shard_map/gather | solution.py:78
  493.5 57.6 %all_to_all.21 = bf16[8,36,3584]{2,1,0:T(8,128)(2,1)} all-to-all(bf16[8,36,3584]{2,1,0:T(8,128)(2,1)} %convert_element_type.48), channel_id=1, replica_groups=mesh['outer'=2,'sec'=8,'tp'=2] {'sec'}, dimensions={0} | all-to-all | bytes 4128768 | tf_op jit(solution)/shard_map/all_to_all | solution.py:79
  555.3 54.0 %all-gather.2.cloned.1.call-done = bf16[288,7168]{1,0:T(8,128)(2,1)} async-done(((bf16[288,3584]{1,0:T(8,128)(2,1)}), bf16[288,7168]{1,0:T(8,128)(2,1)}) %all-gather.2.cloned.1.call-update) | async-done | bytes 4128784 | tf_op jit(solution)/shard_map/all_gather | solution.py:80
  609.2 15.5 %multiply_reduce_fusion.53 = (f32[1536]{0:T(1024)S(1)}, f32[288]{0:T(512)S(1)}, f32[288,1536]{1,0:T(8,128)}) fusion(f32[288]{0:T(512)S(1)} %reshape.171, f32[1536]{0:T(1024)S(1)} %copy-done.10, bf16[288,7168]{1,0:T(8,128)(2,1)} %all-gather.2.cloned.1.call-done, bf16[1536,14336]{1,0:T(8,128)(2,1)} %constant_dynamic-update-slice_fusion, s32[]{:T(128)S(6)} %select_n.26), kind=kOutput, calls=%fused_computation.124 | convolution fusion | flops 6343555072 | bytes 27932932 | tf_op jit(solution)/shard_map/dot_general | solution.py:81
  630.9 7.4 all-reduce.1
  638.4 9.6 %multiply_reduce_fusion.1 = (f32[1536]{0:T(1024)S(1)}, f32[1536]{0:T(1024)S(1)}, f32[1536]{0:T(1024)S(1)}, f32[1536]{0:T(1024)S(1)}, f32[1536]{0:T(1024)S(1)}, /...) fusion(f32[2,12,12,1536]{3,2,1,0:T(8,128)S(1)} %convert_multipl, ...), kind=kLoop, calls=%fused_computation.67 | loop fusion | flops 19436544 | bytes 7200384 | tf_op jit(solution)/shard_map/reduce_sum | solution.py:94
  647.9 6.3 multiply_reduce_fusion.19
  654.3 5.4 multiply_reduce_fusion.38
  665.3 54.4 %all-reduce.7.cloned.1.call-done = f32[51,1536]{1,0:T(8,128)} async-done(((f32[51,1536]{1,0:T(8,128)}), f32[51,1536]{1,0:T(8,128)}) %all-reduce.7.cloned.1.call-update) | async-done | bytes 313360 | tf_op jit(solution)/shard_map/psum | solution.py:100
  721.5 5.5 psum.70
  729.5 5.5 fusion.6
  735.0 20.6 %all-reduce.9.cloned.1.call-done = f32[51,1536]{1,0:T(8,128)} async-done(((f32[51,1536]{1,0:T(8,128)}), f32[51,1536]{1,0:T(8,128)}) %all-reduce.9.cloned.1.call-update) | async-done | bytes 313360 | tf_op jit(solution)/shard_map/psum | solution.py:103
  (144 shorter events, 125.0 us)
Async XLA Ops:
  7.2 106.6 %copy-start.2 = (bf16[2,12,12,1536]{3,0,2,1:T(2,128)(2,1)S(1)}, bf16[2,12,12,1536]{3,0,2,1:T(2,128)(2,1)}, u32[]{:S(2)}) copy-start(bf16[2,12,12,1536]{3,0,2,1:T(2,128)(2,1)} %param.10) | copy-start | bytes 2654212
  7.2 104.5 %copy-start.11 = (s32[2,2]{1,0:T(2,128)S(1)}, s32[2,2]{1,0:T(2,128)}, u32[]{:S(2)}) copy-start(s32[2,2]{1,0:T(2,128)} %param.11) | copy-start | bytes 52
  7.2 376.1 %reduce-scatter.2.cloned.1.call-start = ((), (), s32[]{:S(2)}) async-start(), calls=%async_computation.3 | async-start | bytes 12386304 | tf_op jit(solution)/shard_map/reduce_scatter | solution.py:64
  11.7 35.4 %collective-permute-start = (bf16[1536,896]{1,0:T(8,128)(2,1)}, bf16[1536,896]{1,0:T(8,128)(2,1)S(1)}, u32[]{:S(2)}, u32[]{:S(2)}) collective-permute-start(bf16[1536,896]{1,0:T(8,128)(2,1)} %param.15), channel_id=1, source_target_pairs={{0,2},{2,4},{4,6},{6,8},{8,10},{10,12},{12,14},{14,0},{1,3},{3,5},... | collective-permute-start | bytes 8257544 | tf_op jit(solution)/shard_map/ppermute | solution.py:58
  48.7 63.0 %collective-permute-start.1 = (bf16[1536,896]{1,0:T(8,128)(2,1)S(1)}, bf16[1536,896]{1,0:T(8,128)(2,1)}, u32[]{:S(2)}, u32[]{:S(2)}) collective-permute-start(bf16[1536,896]{1,0:T(8,128)(2,1)S(1)} %collective-permute-done), channel_id=1, source_target_pairs={{0,2},{2,4},{4,6},{6,8},{8,10},{10,12},{12,14},{14,0},{1,3},{3,5},... | collective-permute-start | bytes 8257544 | tf_op jit(solution)/shard_map/ppermute | solution.py:58
  48.7 65.4 %collective-permute-start.4 = (bf16[1536,896]{1,0:T(8,128)(2,1)}, bf16[1536,896]{1,0:T(8,128)(2,1)}, u32[]{:S(2)}, u32[]{:S(2)}) collective-permute-start(bf16[1536,896]{1,0:T(8,128)(2,1)} %param.15), channel_id=1, source_target_pairs={{0,14},{2,0},{4,2},{6,4},{8,6},{10,8},{12,10},{14,12},{1,15},{3,1}... | collective-permute-start | bytes 8257544 | tf_op jit(solution)/shard_map/ppermute | solution.py:60
  111.6 62.3 %collective-permute-start.2 = (bf16[1536,896]{1,0:T(8,128)(2,1)}, bf16[1536,896]{1,0:T(8,128)(2,1)}, u32[]{:S(2)}, u32[]{:S(2)}) collective-permute-start(bf16[1536,896]{1,0:T(8,128)(2,1)} %collective-permute-done.1), channel_id=1, source_target_pairs={{0,2},{2,4},{4,6},{6,8},{8,10},{10,12},{12,14},{14,0},{1,3},{3,5},... | collective-permute-start | bytes 8257544 | tf_op jit(solution)/shard_map/ppermute | solution.py:58
  114.1 92.8 %collective-permute-start.5 = (bf16[1536,896]{1,0:T(8,128)(2,1)}, bf16[1536,896]{1,0:T(8,128)(2,1)}, u32[]{:S(2)}, u32[]{:S(2)}) collective-permute-start(bf16[1536,896]{1,0:T(8,128)(2,1)} %collective-permute-done.4), channel_id=1, source_target_pairs={{0,14},{2,0},{4,2},{6,4},{8,6},{10,8},{12,10},{14,12},{1,15},{3,1}... | collective-permute-start | bytes 8257544 | tf_op jit(solution)/shard_map/ppermute | solution.py:60
  173.9 39.4 %collective-permute-start.3 = (bf16[1536,896]{1,0:T(8,128)(2,1)}, bf16[1536,896]{1,0:T(8,128)(2,1)}, u32[]{:S(2)}, u32[]{:S(2)}) collective-permute-start(bf16[1536,896]{1,0:T(8,128)(2,1)} %collective-permute-done.2), channel_id=1, source_target_pairs={{0,2},{2,4},{4,6},{6,8},{8,10},{10,12},{12,14},{14,0},{1,3},{3,5},... | collective-permute-start | bytes 8257544 | tf_op jit(solution)/shard_map/ppermute | solution.py:58
  206.8 1.9 copy-start.5
  206.8 1.9 copy-start.7
  206.8 32.8 %collective-permute-start.6 = (bf16[1536,896]{1,0:T(8,128)(2,1)}, bf16[1536,896]{1,0:T(8,128)(2,1)}, u32[]{:S(2)}, u32[]{:S(2)}) collective-permute-start(bf16[1536,896]{1,0:T(8,128)(2,1)} %collective-permute-done.5), channel_id=1, source_target_pairs={{0,14},{2,0},{4,2},{6,4},{8,6},{10,8},{12,10},{14,12},{1,15},{3,1}... | collective-permute-start | bytes 8257544 | tf_op jit(solution)/shard_map/ppermute | solution.py:60
  220.7 3.8 copy-start.1
  266.8 3.8 copy-start.4
  391.0 5.3 copy-start.12
  391.0 58.1 %all-to-all-start = ((bf16[8,36,3584]{2,1,0:T(8,128)(2,1)}), bf16[8,36,3584]{2,1,0:T(8,128)(2,1)}, u32[]{:S(2)}, u32[]{:S(2)}) async-start(bf16[8,36,3584]{2,1,0:T(8,128)(2,1)} %all_to_all.14), calls=%async_computation.1 | async-start | bytes 4587520 | tf_op jit(solution)/shard_map/all_to_all | solution.py:67
  395.7 213.5 %all-gather.2.cloned.1.call-start = ((), (), s32[]{:S(2)}) async-start(), calls=%async_computation.4 | async-start | bytes 6193152 | tf_op jit(solution)/shard_map/all_gather | solution.py:80
  453.1 9.2 %copy-start.9 = (f32[3584]{0:T(1024)S(1)}, f32[3584]{0:T(1024)}, u32[]{:S(2)}) copy-start(f32[3584]{0:T(1024)} %param.18) | copy-start | bytes 43012
  551.2 58.1 %copy-start.10 = (f32[1536]{0:T(1024)S(1)}, f32[1536]{0:T(1024)}, u32[]{:S(2)}) copy-start(f32[1536]{0:T(1024)} %param.13) | copy-start | bytes 18436
  555.1 164.7 %all-reduce.7.cloned.1.call-start = ((), (), s32[]{:S(2)}) async-start(), calls=%async_computation.5 | async-start | bytes 688128 | tf_op jit(solution)/shard_map/psum | solution.py:100
  624.7 2.8 copy-start.6
  624.7 2.8 copy-start.8
  647.9 6.4 copy-start.3
  665.3 90.3 %all-reduce.9.cloned.1.call-start = ((), (), s32[]{:S(2)}) async-start(), calls=%async_computation.6 | async-start | bytes 688128 | tf_op jit(solution)/shard_map/psum | solution.py:103
  (1 other events, 1.5 us)
Sparse Core Ops, SparseCore 0:
  284.7 98.5 reduce-scatter.1
  555.3 53.9 all-gather.1
  665.4 54.3 all-reduce.6
  729.6 25.9 all-reduce.8
